TPU v7x, 32 devices: a whole 2x2x4 slice. The times are simulated.
32 devices in a mesh: shard: 2 (over x), ctx: 4 (over y, core), tp: 4 (over z).
Axes of the slice: x: 2, y: 2, z: 4, core: 2. Of those that a mesh axis runs over, the one named last changes fastest.
Arguments:
- inputs: bfloat16 [4, 1536, 768], P('shard', 'ctx'), may hold values from -6 to 6
- cotangent: bfloat16 [4, 1536, 768], P('shard', 'ctx'), may hold values from -6 to 6
- ln1_gain: float32 [768], replicated, may hold values from 0.25 to 1.75
- ln1_bias: float32 [768], replicated, may hold values from -4 to 4
- w_qkv: bfloat16 [3, 768, 768], P(None, 'shard', 'tp'), may hold values from -0.21875 to 0.21875
- q_bias: float32 [768], P('tp'), may hold values from -6 to 6
- v_bias: float32 [768], P('tp'), may hold values from -1.5 to 1.5
- w_out: bfloat16 [768, 768], P('tp', 'shard'), may hold values from -2.5 to 2.5
- out_bias: float32 [768], replicated, may hold values from -4 to 4
- ln2_gain: float32 [768], replicated, may hold values from 0.25 to 1.75
- ln2_bias: float32 [768], replicated, may hold values from -4 to 4
- w_up: bfloat16 [768, 3072], P('shard', 'tp'), may hold values from -0.21875 to 0.21875
- up_bias: float32 [3072], P('tp'), may hold values from -6 to 6
- w_down: bfloat16 [3072, 768], P('tp', 'shard'), may hold values from -0.109375 to 0.109375
- down_bias: float32 [768], replicated, may hold values from -4 to 4
Outputs:
- output: bfloat16 [4, 1536, 768], P('shard', 'ctx')
- grad_inputs: bfloat16 [4, 1536, 768], P('shard', 'ctx')
- grad_ln1_gain: float32 [768], replicated
- grad_ln1_bias: float32 [768], replicated
- grad_qkv: float32 [3, 768, 768], P(None, 'shard', 'tp')
- grad_q_bias: float32 [768], P('tp')
- grad_v_bias: float32 [768], P('tp')
- grad_w_out: float32 [768, 768], P('tp', 'shard')
- grad_out_bias: float32 [768], replicated
- grad_ln2_gain: float32 [768], replicated
- grad_ln2_bias: float32 [768], replicated
- grad_w_up: float32 [768, 3072], P('shard', 'tp')
- grad_up_bias: float32 [3072], P('tp')
- grad_w_down: float32 [3072, 768], P('tp', 'shard')
- grad_down_bias: float32 [768], replicated
All inputs are finite; a program needn't handle non-finite values.
Results may differ from a plain program's by a relative error of at most 0.02.
Values may be sent and summed in bfloat16 or wider, within the bound.
A program may use at most 128 MiB of HBM per device.

v0:
```python
import jax
import jax.numpy as jnp
from jax import lax
from jax.sharding import PartitionSpec as P

HEAD_DIM = 64
norm_eps = 1e-05
inv_root_two = 0.7071067811865476
inv_root_tau = 0.3989422804014327


def norm_rows(inputs_f, gain_vec, bias_vec):
    row_mean = jnp.mean(inputs_f, -1, keepdims=True)
    centred = inputs_f - row_mean
    row_var = jnp.mean(centred * centred, -1, keepdims=True)
    inv_std = lax.rsqrt(row_var + norm_eps)
    unit_rows = centred * inv_std
    return (unit_rows * gain_vec + bias_vec, unit_rows, inv_std)


def norm_back(upstream, unit_rows, inv_std, gain_vec):
    scaled = upstream * gain_vec
    inner = (
        scaled
        - jnp.mean(scaled, -1, keepdims=True)
        - unit_rows * jnp.mean(scaled * unit_rows, -1, keepdims=True)
    )
    return inv_std * inner


def gelu_slope(pre_act):
    cumulative = 0.5 * (1.0 + lax.erf(pre_act * inv_root_two))
    density = jnp.exp(-0.5 * pre_act * pre_act) * inv_root_tau
    return cumulative + pre_act * density


def tp_total(values):
    return lax.psum(values.astype(jnp.bfloat16), "tp").astype(jnp.float32)


def shards(
    inputs,
    cotangent,
    ln1_gain,
    ln1_bias,
    w_qkv,
    q_bias,
    v_bias,
    w_out,
    out_bias,
    ln2_gain,
    ln2_bias,
    w_up,
    up_bias,
    w_down,
    down_bias,
):
    clip_count, block_len, model_width = inputs.shape
    count_of_rows = clip_count * block_len
    share_rows = count_of_rows // lax.axis_size("tp")
    share_start = lax.axis_index("tp") * share_rows

    def rows_part(values):
        return lax.dynamic_slice_in_dim(values, share_start, share_rows, 0)

    wqkv_full, wout_full, wup_full, wdown_full = (
        lax.all_gather(w_qkv, "shard", axis=1, tiled=True),
        lax.all_gather(w_out, "shard", axis=1, tiled=True),
        lax.all_gather(w_up, "shard", axis=0, tiled=True),
        lax.all_gather(w_down, "shard", axis=1, tiled=True),
    )
    shard_local_width = wqkv_full.shape[2]
    heads_local = shard_local_width // HEAD_DIM
    attn_scale = HEAD_DIM ** (-0.5)
    x_rows = inputs.astype(jnp.float32).reshape(count_of_rows, model_width)
    normed_one, unit_one, inv_one = norm_rows(x_rows, ln1_gain, ln1_bias)
    act_one = normed_one.astype(jnp.bfloat16)
    projected = jnp.einsum("rd,kdc->krc", act_one, wqkv_full, preferred_element_type=jnp.float32)
    queries = (projected[0] + q_bias).astype(jnp.bfloat16)
    key_rows = projected[1].astype(jnp.bfloat16)
    value_rows = (projected[2] + v_bias).astype(jnp.bfloat16)
    q_heads = queries.reshape(clip_count, block_len, heads_local, HEAD_DIM)
    key_blocks = key_rows.reshape(clip_count, block_len, shard_local_width)
    value_blocks = value_rows.reshape(clip_count, block_len, shard_local_width)
    run_max = jnp.full((clip_count, heads_local, block_len), -1e30, jnp.float32)
    key_piece = lax.all_gather(key_blocks, "ctx", axis=1, tiled=True)
    value_piece = lax.all_gather(value_blocks, "ctx", axis=1, tiled=True)
    piece_len = key_piece.shape[1]
    key_heads = key_piece.reshape(clip_count, piece_len, heads_local, HEAD_DIM)
    value_heads = value_piece.reshape(clip_count, piece_len, heads_local, HEAD_DIM)
    scores = (
        jnp.einsum("cqhe,cnhe->chqn", q_heads, key_heads, preferred_element_type=jnp.float32)
        * attn_scale
    )
    new_max = jnp.maximum(run_max, jnp.max(scores, -1))
    expo = jnp.exp(scores - new_max[..., None])
    run_sum = jnp.sum(expo, -1)
    weighted = jnp.einsum(
        "chqn,cnhe->chqe",
        expo.astype(jnp.bfloat16),
        value_heads,
        preferred_element_type=jnp.float32,
    )
    run_max, run_sum, weighted = (new_max, run_sum, weighted)
    log_norm = run_max + jnp.log(run_sum)
    attn_heads = jnp.transpose(weighted / run_sum[..., None], (0, 2, 1, 3))
    attn_rows = attn_heads.reshape(count_of_rows, shard_local_width)
    attn_low = attn_rows.astype(jnp.bfloat16)
    attn_term = jnp.dot(attn_low, wout_full, preferred_element_type=jnp.float32)
    residual = x_rows + tp_total(attn_term) + out_bias
    normed_two, unit_two, inv_two = norm_rows(residual, ln2_gain, ln2_bias)
    act_two = normed_two.astype(jnp.bfloat16)
    hidden_pre = jnp.dot(act_two, wup_full, preferred_element_type=jnp.float32) + up_bias
    hidden = jax.nn.gelu(hidden_pre, approximate=False).astype(jnp.bfloat16)
    branch_term = jnp.dot(hidden, wdown_full, preferred_element_type=jnp.float32)
    output = (
        (residual + tp_total(branch_term) + down_bias)
        .astype(jnp.bfloat16)
        .reshape(clip_count, block_len, model_width)
    )
    wqkv_full, wout_full, wup_full, wdown_full = (
        lax.all_gather(w_qkv, "shard", axis=1, tiled=True),
        lax.all_gather(w_out, "shard", axis=1, tiled=True),
        lax.all_gather(w_up, "shard", axis=0, tiled=True),
        lax.all_gather(w_down, "shard", axis=1, tiled=True),
    )
    grad_y = cotangent.astype(jnp.float32).reshape(count_of_rows, model_width)
    grad_db = jnp.sum(rows_part(grad_y), 0)
    grad_ylow = grad_y.astype(jnp.bfloat16)
    grad_wdown = jnp.einsum("rf,rd->fd", hidden, grad_ylow, preferred_element_type=jnp.float32)
    grad_hidden = jnp.einsum("rd,fd->rf", grad_ylow, wdown_full, preferred_element_type=jnp.float32)
    grad_pre = (grad_hidden * gelu_slope(hidden_pre)).astype(jnp.bfloat16)
    grad_ub = jnp.sum(grad_pre.astype(jnp.float32), 0)
    grad_wup = jnp.einsum("rd,rf->df", act_two, grad_pre, preferred_element_type=jnp.float32)
    acttwo_term = jnp.einsum("rf,df->rd", grad_pre, wup_full, preferred_element_type=jnp.float32)
    grad_acttwo = tp_total(acttwo_term)
    grad_resid = grad_y + norm_back(grad_acttwo, unit_two, inv_two, ln2_gain)
    grad_g2 = jnp.sum(rows_part(grad_acttwo) * rows_part(unit_two), 0)
    grad_b2 = jnp.sum(rows_part(grad_acttwo), 0)
    grad_ob = jnp.sum(rows_part(grad_resid), 0)
    grad_mixed = grad_resid.astype(jnp.bfloat16)
    grad_wout = jnp.einsum("rc,rd->cd", attn_low, grad_mixed, preferred_element_type=jnp.float32)
    grad_attn = jnp.einsum(
        "rd,cd->rc", grad_mixed, wout_full, preferred_element_type=jnp.float32
    ).astype(jnp.bfloat16)
    grad_heads = grad_attn.reshape(clip_count, block_len, heads_local, HEAD_DIM)
    row_dots = jnp.transpose(jnp.sum(grad_heads.astype(jnp.float32) * attn_heads, -1), (0, 2, 1))
    key_piece = lax.all_gather(key_blocks, "ctx", axis=1, tiled=True)
    value_piece = lax.all_gather(value_blocks, "ctx", axis=1, tiled=True)
    piece_len = key_piece.shape[1]
    key_heads = key_piece.reshape(clip_count, piece_len, heads_local, HEAD_DIM)
    value_heads = value_piece.reshape(clip_count, piece_len, heads_local, HEAD_DIM)
    scores = (
        jnp.einsum("cqhe,cnhe->chqn", q_heads, key_heads, preferred_element_type=jnp.float32)
        * attn_scale
    )
    probs = jnp.exp(scores - log_norm[..., None])
    grad_prob = jnp.einsum(
        "cqhe,cnhe->chqn", grad_heads, value_heads, preferred_element_type=jnp.float32
    )
    grad_score = (probs * (grad_prob - row_dots[..., None])).astype(jnp.bfloat16)
    grad_query = (
        jnp.einsum("chqn,cnhe->chqe", grad_score, key_heads, preferred_element_type=jnp.float32)
        * attn_scale
    )
    piece_key = (
        jnp.einsum("chqn,cqhe->cnhe", grad_score, q_heads, preferred_element_type=jnp.float32)
        * attn_scale
    )
    piece_value = jnp.einsum(
        "chqn,cqhe->cnhe",
        probs.astype(jnp.bfloat16),
        grad_heads,
        preferred_element_type=jnp.float32,
    )
    joined = jnp.concatenate(
        [
            piece_key.reshape(clip_count, piece_len, shard_local_width),
            piece_value.reshape(clip_count, piece_len, shard_local_width),
        ],
        -1,
    )
    grad_kv = joined
    grad_query, grad_kv = (grad_query, grad_kv)
    key_value_totals = lax.psum_scatter(
        grad_kv.astype(jnp.bfloat16), "ctx", scatter_dimension=1, tiled=True
    ).astype(jnp.float32)
    query_gradient_partial = (
        jnp.transpose(grad_query, (0, 2, 1, 3))
        .reshape(count_of_rows, shard_local_width)
        .astype(jnp.bfloat16)
    )
    key_gradient_partial = (
        key_value_totals[:, :, :shard_local_width]
        .reshape(count_of_rows, shard_local_width)
        .astype(jnp.bfloat16)
    )
    value_gradient_partial = (
        key_value_totals[:, :, shard_local_width:]
        .reshape(count_of_rows, shard_local_width)
        .astype(jnp.bfloat16)
    )
    stacked_tensors = jnp.stack(
        [query_gradient_partial, key_gradient_partial, value_gradient_partial]
    )
    grad_qb = jnp.sum(query_gradient_partial.astype(jnp.float32), 0)
    grad_vb = jnp.sum(value_gradient_partial.astype(jnp.float32), 0)
    grad_wqkv = jnp.einsum(
        "krc,rd->kdc", stacked_tensors, act_one, preferred_element_type=jnp.float32
    )
    actone_term = jnp.einsum(
        "krc,kdc->rd", stacked_tensors, wqkv_full, preferred_element_type=jnp.float32
    )
    grad_actone = tp_total(actone_term)
    input_norm = norm_back(grad_actone, unit_one, inv_one, ln1_gain)
    grad_g1 = jnp.sum(rows_part(grad_actone) * rows_part(unit_one), 0)
    grad_b1 = jnp.sum(rows_part(grad_actone), 0)
    grad_inputs = (
        (grad_resid + input_norm).astype(jnp.bfloat16).reshape(clip_count, block_len, model_width)
    )
    partial_set = (
        lax.psum_scatter(
            grad_wqkv.astype(jnp.bfloat16), "shard", scatter_dimension=1, tiled=True
        ).astype(jnp.float32),
        lax.psum_scatter(
            grad_wout.astype(jnp.bfloat16), "shard", scatter_dimension=1, tiled=True
        ).astype(jnp.float32),
        lax.psum_scatter(
            grad_wup.astype(jnp.bfloat16), "shard", scatter_dimension=0, tiled=True
        ).astype(jnp.float32),
        lax.psum_scatter(
            grad_wdown.astype(jnp.bfloat16), "shard", scatter_dimension=1, tiled=True
        ).astype(jnp.float32),
    )
    owned = (
        lax.psum(partial_set[0].astype(jnp.bfloat16), "ctx").astype(jnp.float32),
        lax.psum(partial_set[1].astype(jnp.bfloat16), "ctx").astype(jnp.float32),
        lax.psum(partial_set[2].astype(jnp.bfloat16), "ctx").astype(jnp.float32),
        lax.psum(partial_set[3].astype(jnp.bfloat16), "ctx").astype(jnp.float32),
    )
    vectors = lax.psum((grad_qb, grad_vb, grad_ub), ("shard", "ctx"))
    norm_sums = lax.psum(
        (grad_g1, grad_b1, grad_ob, grad_g2, grad_b2, grad_db), ("shard", "ctx", "tp")
    )
    return (
        output,
        grad_inputs,
        norm_sums[0],
        norm_sums[1],
        owned[0],
        vectors[0],
        vectors[1],
        owned[1],
        norm_sums[2],
        norm_sums[3],
        norm_sums[4],
        owned[2],
        vectors[2],
        owned[3],
        norm_sums[5],
    )


def solution(mesh):
    placed = (
        P("shard", "ctx", None),
        P("shard", "ctx", None),
        P(),
        P(),
        P(None, "shard", "tp"),
        P("tp"),
        P("tp"),
        P("tp", "shard"),
        P(),
        P(),
        P(),
        P("shard", "tp"),
        P("tp"),
        P("tp", "shard"),
        P(),
    )
    return jax.shard_map(
        shards,
        mesh=mesh,
        in_specs=placed,
        out_specs=(
            P("shard", "ctx", None),
            P("shard", "ctx", None),
            P(),
            P(),
            P(None, "shard", "tp"),
            P("tp"),
            P("tp"),
            P("tp", "shard"),
            P(),
            P(),
            P(),
            P("shard", "tp"),
            P("tp"),
            P("tp", "shard"),
            P(),
        ),
        check_vma=False,
    )
```

profile of v0, /device:TPU:0, one launch (start us, length us, event | category | flops | bytes accessed | tf_op | source)
XLA Modules:
  0.0 535.8 jit_solution(14505202180377104426)
XLA Ops:
  8.1 1.6 convert_reduce_fusion
  9.7 1.7 fusion.23
  11.5 13.8 %all_gather.24 = bf16[3,768,192]{1,2,0:T(8,128)(2,1)S(1)} all-gather(bf16[3,384,192]{1,2,0:T(8,128)(2,1)S(1)} %copy-done.21), channel_id=1, replica_groups=mesh['shard'=2,'ctx'=4,'tp'=4] {'shard'}, dimensions={1}, use_global_device_ids=true | all-gather | bytes 1327104 | tf_op jit(solution)/shard_map/all_gather | solution.py:67
  32.5 5.8 %all_gather.27 = bf16[192,768]{1,0:T(8,128)(2,1)S(1)} all-gather(bf16[192,384]{1,0:T(8,128)(2,1)S(1)} %copy-done.22), channel_id=1, replica_groups=mesh['shard'=2,'ctx'=4,'tp'=4] {'shard'}, dimensions={1}, use_global_device_ids=true | all-gather | bytes 442368 | tf_op jit(solution)/shard_map/all_gather | solution.py:68
  38.3 10.2 %all-gather.5.cloned.1.call-done = bf16[2,1536,192]{1,0,2:T(2,128)(2,1)} async-done(((bf16[2,384,192]{1,0,2:T(2,128)(2,1)}), bf16[2,1536,192]{1,0,2:T(2,128)(2,1)}) %all-gather.5.cloned.1.call-update) | async-done | bytes 1179664 | tf_op jit(solution)/shard_map/all_gather | solution.py:86
  49.9 7.2 %multiply_reduce_fusion = (f32[2,3,384]{2,1,0:T(4,128)S(1)}, f32[2,3,384,1536]{3,2,1,0:T(8,128)}) fusion(bf16[2,1536,3,64]{1,3,2,0:T(8,128)(2,1)S(1)} %bitcast.108, f32[2,384,3,64]{1,0,3,2:T(2,128)S(1)} %squeeze.7, f32[3,64]{1,0:T(4,128)S(1)} %add.159), kind=kOutput, calls=%fused_computation.6 | convolution fusion | flops 460355328 | bytes 15935232 | tf_op jit(solution)/shard_map/cqhe,cnhe->chqn/dot_general | solution.py:92
  57.1 7.7 %fusion = f32[2,3,384]{2,1,0:T(4,128)S(1)} fusion(f32[2,3,384,1536]{3,2,1,0:T(8,128)} %get-tuple-element.45, f32[2,3,384]{2,1,0:T(4,128)S(1)} %broadcast_maximum_fusion), kind=kLoop, calls=%fused_computation.3 | loop fusion | flops 10614528 | bytes 14174208 | tf_op jit(solution)/shard_map/reduce_sum | solution.py:97
  64.8 3.4 all-gather.7.cloned.1.call-done
  69.7 8.9 %fusion.56 = (bf16[2,384,3,64]{1,3,2,0:T(8,128)(2,1)S(1)}, f32[2,384,3,64]{1,3,2,0:T(8,128)}) fusion(f32[2,384,3]{1,2,0:T(4,128)S(1)} %bitcast.137, bf16[2,1536,3,64]{1,3,2,0:T(8,128)(2,1)S(1)} %bitcast.114, f32[2,3,384,1536]{3,2,1,0:T(8,128)} %get-tuple-element.45, f32[2,3,384]{2,1,0:T(4,128)S(1)} %broadcast_maximum_fusion), kind=kOutput, calls=%fused_computation.114 | convolution fusion | flops 463896576 | bytes 16238592 | tf_op jit(solution)/shard_map/chqn,cnhe->chqe/dot_general | solution.py:98
  79.0 1.5 convolution_convert_fusion.4
  81.7 11.2 %all-reduce.11.cloned.1.call-start = ((), (), s32[]{:S(2)}) async-start(), calls=%async_computation.10 | async-start | bytes 2359296 | tf_op jit(solution)/shard_map/psum | solution.py:38
  92.9 43.7 %all-reduce.9.cloned.1.call-done = bf16[768,768]{1,0:T(8,128)(2,1)} async-done(((bf16[768,768]{1,0:T(8,128)(2,1)}), bf16[768,768]{1,0:T(8,128)(2,1)}) %all-reduce.9.cloned.1.call-update) | async-done | bytes 1179664 | tf_op jit(solution)/shard_map/psum | solution.py:38
  136.6 1.8 fusion.33
  140.5 8.9 %fusion.15 = (bf16[768,768]{1,0:T(8,128)(2,1)}, f32[768,768]{1,0:T(8,128)}) fusion(f32[768]{0:T(1024)S(1)} %copy-done.42, bf16[768,768]{1,0:T(8,128)(2,1)} %all-gather.9.cloned.1.call-done, f32[768,768]{1,0:T(8,128)S(1)} %subtract_multiply_fusion, f32[768]{0:T(1024)} %param.25, f32[768]{0:T(1024)S(1)} %copy-done.36), kind=kOutput, calls=%fused_computation.18 | convolution fusion | flops 946667520 | bytes 7087104 | tf_op jit(solution)/shard_map/dot_general | solution.py:113
  149.4 4.7 convert_reduce_fusion.1
  155.1 2.1 convolution_convert_fusion.2
  158.1 54.8 %all-reduce.11.cloned.1.call-done = bf16[768,768]{1,0:T(8,128)(2,1)} async-done(((bf16[768,768]{1,0:T(8,128)(2,1)}), bf16[768,768]{1,0:T(8,128)(2,1)}) %all-reduce.11.cloned.1.call-update) | async-done | bytes 1179664 | tf_op jit(solution)/shard_map/psum | solution.py:38
  212.9 1.9 multiply_reduce_fusion.5
  214.9 2.4 multiply_add_fusion
  218.6 1.7 reshape.206
  221.6 7.9 %fusion.9 = bf16[2,3,64,1536]{3,2,1,0:T(8,128)(2,1)S(1)} fusion(f32[2,3,384,1536]{3,2,1,0:T(8,128)} %get-tuple-element.45, f32[2,3,384]{2,1,0:T(4,128)S(1)} %log_add_fusion, bf16[2,384,3,64]{1,0,3,2:T(2,128)(2,1)} %reshape.206), kind=kOutput, calls=%fused_computation.14 | convolution fusion | flops 464191488 | bytes 15639552 | tf_op jit(solution)/shard_map/chqn,cqhe->cnhe/dot_general | solution.py:170
  229.5 7.1 %multiply_convert_fusion = bf16[2,3,384,1536]{3,2,1,0:T(8,128)(2,1)S(1)} fusion(f32[2,3,384,1536]{3,2,1,0:T(8,128)} %get-tuple-element.45, bf16[2,1536,3,64]{1,3,2,0:T(8,128)(2,1)S(1)} %bitcast.115, f32[2,3,384]{2,1,0:T(4,128)S(1)} %bitcast.136, f32[2,3,384]{2,1,0:T(4,128)S(1)} %log_add_fusion, bf16[2,384,3,64]{1,0,3,2:T(2,128)(2,1)S(1)} %copy-done.12), kind=kOutput, calls=%fused_computation | convolution fusion | flops 470679552 | bytes 22726656 | tf_op jit(solution)/shard_map/cqhe,cnhe->chqn/dot_general | solution.py:158
  238.0 1.5 copy-done
  239.5 1.6 pad_maximum_fusion
  241.1 6.8 %copy.55 = bf16[2,1536,384]{2,0,1:T(2,128)(2,1)} copy(bf16[2,1536,384]{1,2,0:T(8,128)(2,1)} %pad_maximum_fusion) | data formatting | bytes 4718592
  248.0 3.6 copy.68
  251.6 2.1 convolution_convert_fusion.5
  253.7 1.9 copy.59
  255.7 4.1 convolution_convert_fusion
  259.8 2.4 copy.61
  262.5 5.6 %convert_reduce_fusion.3 = (f32[3,64]{1,0:T(4,128)S(1)}, bf16[2,3,384,64]{2,3,1,0:T(8,128)(2,1)S(1)}) fusion(bf16[2,3,384,1536]{3,2,1,0:T(8,128)(2,1)} %copy-done, bf16[2,1536,3,64]{1,3,2,0:T(8,128)(2,1)} %bitcast.109), kind=kOutput, calls=%fused_computation.82 | convolution fusion | flops 453574464 | bytes 8553216 | tf_op jit(solution)/shard_map/chqn,cnhe->chqe/dot_general | solution.py:163
  269.1 1.9 convert_element_type.198
  271.0 1.7 constant_dynamic-update-slice_fusion.2
  272.7 11.7 %reduce-scatter.16.cloned.1.call-done = bf16[384,768]{1,0:T(8,128)(2,1)} async-done(((bf16[1536,768]{1,0:T(8,128)(2,1)}), bf16[384,768]{1,0:T(8,128)(2,1)}) %reduce-scatter.16.cloned.1.call-update) | async-done | bytes 589840
  284.4 2.5 reshape.216
  286.9 2.8 fusion.55
  289.7 2.0 copy.53
  291.7 1.9 convert_element_type.200
  293.6 2.0 copy.54
  295.6 1.9 convert_element_type.201
  297.4 1.7 constant_dynamic-update-slice_fusion.1
  299.1 1.7 constant_dynamic-update-slice_fusion
  300.8 2.8 fusion.44
  304.6 3.5 copy.57
  308.1 4.1 reshape.217
  312.3 4.1 convolution_convert_fusion.1
  316.5 3.9 convolution_convert_fusion.3
  320.4 2.1 bitcast_convert_fusion
  327.5 1.8 dynamic-slice_reduce_fusion.2
  329.3 1.7 copy.60
  331.0 2.1 copy.62
  333.1 1.9 copy.64
  336.1 14.2 %all-reduce.1 = (f32[192]{0:T(256)}, f32[192]{0:T(256)}, f32[768]{0:T(1024)}) all-reduce(f32[192]{0:T(256)} %reduce_sum.186, f32[192]{0:T(256)S(1)} %convert_reduce_fusion.2, f32[768]{0:T(1024)} %get-tuple-element.52), channel_id=1, replica_groups=mesh['shard'=2,'ctx'=4,'tp'=4] {'shard','ctx'}, use_global_device_ids=true, to_apply=%region_23.0 | all-reduce | flops 1152 | bytes 9216 | tf_op jit(solution)/shard_map/psum | solution.py:241
  350.3 2.5 reshape.218
  352.9 2.1 copy.58
  355.0 16.1 %reduce-scatter.14.cloned.1.call-done = bf16[384,768]{1,0:T(8,128)(2,1)} async-done(((bf16[768,768]{1,0:T(8,128)(2,1)}), bf16[384,768]{1,0:T(8,128)(2,1)}) %reduce-scatter.14.cloned.1.call-update) | async-done | bytes 589840 | tf_op jit(solution)/shard_map/reduce_scatter | solution.py:228
  371.1 99.0 %all-reduce.13.cloned.1.call-done = (bf16[768,768]{1,0:T(8,128)(2,1)}, bf16[768,768]{1,0:T(8,128)(2,1)}) async-done(((bf16[768,768]{1,0:T(8,128)(2,1)}, bf16[768,768]{1,0:T(8,128)(2,1)}), (bf16[768,768]{1,0:T(8,128)(2,1)}, bf16[768,768]{1,0:T(8,128)(2,1)})) %all-reduce.13.cloned.1.call-update) | async-done | bytes 2359312 | tf_op jit(solution)/shard_map/psum | solution.py:38
  470.1 2.9 multiply_reduce_fusion.4
  473.1 1.8 dynamic-slice_reduce_fusion.3
  474.9 41.0 %all-reduce = (f32[768]{0:T(1024)}, f32[768]{0:T(1024)}, f32[768]{0:T(1024)}, f32[768]{0:T(1024)}, f32[768]{0:T(1024)}, /*index=5*/f32[768]{0:T(1024)}) all-reduce(f32[768]{0:T(1024)} %get-tuple-element.18, f32[768]{0:T(1024)} %get-tuple-element.17, ...), channel_id=1, replica_groups=mesh['shard'=2,'ctx'=4,'tp'=4] {'shard','ctx','tp'}, use_global_device_ids=true, to_apply=%region_17.0 | all-reduce | flops 4608 | bytes 36864 | tf_op jit(solution)/shard_map/psum | solution.py:242
  517.3 4.0 add_convert_fusion
  521.3 1.7 convert_element_type.211
  523.0 2.0 convert_element_type.207
  525.0 2.2 convert_element_type.213
  (163 shorter events, 30.4 us)
Async XLA Ops:
  8.0 17.3 %copy-start.1 = (bf16[2,384,768]{2,1,0:T(8,128)(2,1)S(1)}, bf16[2,384,768]{2,1,0:T(8,128)(2,1)}, u32[]{:S(2)}) copy-start(bf16[2,384,768]{2,1,0:T(8,128)(2,1)} %param.15) | copy-start | bytes 3538948
  8.0 3.5 copy-start.21
  8.0 40.5 %all-gather.5.cloned.1.call-start = ((), (), s32[]{:S(2)}) async-start(), calls=%async_computation.5 | async-start | bytes 1474560 | tf_op jit(solution)/shard_map/all_gather | solution.py:86
  11.5 14.3 %copy-start.25 = (f32[768]{0:T(1024)}, f32[768]{0:T(1024)S(1)}, u32[]{:S(2)}) copy-start(f32[768]{0:T(1024)S(1)} %div.38) | copy-start | bytes 9220
  11.5 14.2 %copy-start.27 = (f32[768]{0:T(1024)}, f32[768]{0:T(1024)S(1)}, u32[]{:S(2)}) copy-start(f32[768]{0:T(1024)S(1)} %rsqrt.20) | copy-start | bytes 9220
  11.5 14.2 %copy-start.34 = (f32[768]{0:T(1024)S(1)}, f32[768]{0:T(1024)}, u32[]{:S(2)}) copy-start(f32[768]{0:T(1024)} %param.17) | copy-start | bytes 9220
  11.5 14.2 %copy-start.43 = (f32[768]{0:T(1024)S(1)}, f32[768]{0:T(1024)}, u32[]{:S(2)}) copy-start(f32[768]{0:T(1024)} %param.18) | copy-start | bytes 9220
  25.3 1.4 copy-start.18
  25.8 1.4 copy-start.13
  27.2 1.2 copy-start.17
  28.4 2.5 copy-start.40
  29.3 2.8 copy-start.39
  29.3 39.0 %all-gather.7.cloned.1.call-start = ((), (), s32[]{:S(2)}) async-start(), calls=%async_computation.6 | async-start | bytes 1474560 | tf_op jit(solution)/shard_map/all_gather | solution.py:87
  30.6 1.8 copy-start.22
  32.0 104.6 %all-reduce.9.cloned.1.call-start = ((), (), s32[]{:S(2)}) async-start(), calls=%async_computation.7 | async-start | bytes 2359296 | tf_op jit(solution)/shard_map/psum | solution.py:38
  32.5 24.6 %copy-start.7 = (f32[2,384,3,64]{1,0,3,2:T(2,128)}, f32[2,384,3,64]{1,0,3,2:T(2,128)S(1)}, u32[]{:S(2)}) copy-start(f32[2,384,3,64]{1,0,3,2:T(2,128)S(1)} %squeeze.7) | copy-start | bytes 1769476
  38.3 40.7 %copy-start.15 = (bf16[192,768]{1,0:T(8,128)(2,1)}, bf16[192,768]{1,0:T(8,128)(2,1)S(1)}, u32[]{:S(2)}) copy-start(bf16[192,768]{1,0:T(8,128)(2,1)S(1)} %all_gather.27) | copy-start | bytes 884740
  49.9 7.2 %copy-start.4 = (bf16[2,1536,192]{1,2,0:T(8,128)(2,1)}, bf16[2,1536,192]{1,2,0:T(8,128)(2,1)S(1)}, u32[]{:S(2)}) copy-start(bf16[2,1536,192]{1,2,0:T(8,128)(2,1)S(1)} %copy.46) | copy-start | bytes 3538948
  57.1 7.7 %copy-start.23 = (f32[2,3,384]{2,1,0:T(4,128)}, f32[2,3,384]{2,1,0:T(4,128)S(1)}, u32[]{:S(2)}) copy-start(f32[2,3,384]{2,1,0:T(4,128)S(1)} %get-tuple-element.44) | copy-start | bytes 27652
  64.8 13.8 %copy-start.31 = (f32[2,3,384]{2,1,0:T(4,128)}, f32[2,3,384]{2,1,0:T(4,128)S(1)}, u32[]{:S(2)}) copy-start(f32[2,3,384]{2,1,0:T(4,128)S(1)} %fusion) | copy-start | bytes 27652
  69.7 9.0 %copy-start.9 = (bf16[2,1536,192]{1,2,0:T(8,128)(2,1)}, bf16[2,1536,192]{1,2,0:T(8,128)(2,1)S(1)}, u32[]{:S(2)}) copy-start(bf16[2,1536,192]{1,2,0:T(8,128)(2,1)S(1)} %copy.47) | copy-start | bytes 3538948
  78.9 57.7 %copy-start.29 = (f32[768]{0:T(1024)S(1)}, f32[768]{0:T(1024)}, u32[]{:S(2)}) copy-start(f32[768]{0:T(1024)} %param.23) | copy-start | bytes 9220
  79.0 59.5 %copy-start.14 = (bf16[24,8,2,384]{3,1,2,0:T(8,128)(2,1)}, bf16[24,8,2,384]{3,1,2,0:T(8,128)(2,1)S(1)}, u32[]{:S(2)}) copy-start(bf16[24,8,2,384]{3,1,2,0:T(8,128)(2,1)S(1)} %copy.67) | copy-start | bytes 884740
  80.6 59.7 %all-gather.9.cloned.1.call-start = ((), (), s32[]{:S(2)}) async-start(), calls=%async_computation.8 | async-start | bytes 1769472 | tf_op jit(solution)/shard_map/all_gather | solution.py:69
  81.2 68.3 %all-gather.11.cloned.1.call-start = ((), (), s32[]{:S(2)}) async-start(), calls=%async_computation.9 | async-start | bytes 1769472 | tf_op jit(solution)/shard_map/all_gather | solution.py:70
  81.7 131.1 %all-reduce.11.cloned.1.call-start = ((), (), s32[]{:S(2)}) async-start(), calls=%async_computation.10 | async-start | bytes 2359296 | tf_op jit(solution)/shard_map/psum | solution.py:38
  136.6 1.8 copy-start.3
  139.2 0.6 copy-start.32
  139.8 0.7 copy-start.36
  139.8 0.7 copy-start.42
  140.3 72.6 %copy-start.2 = (f32[768,768]{1,0:T(8,128)}, f32[768,768]{1,0:T(8,128)S(1)}, u32[]{:S(2)}) copy-start(f32[768,768]{1,0:T(8,128)S(1)} %subtract_multiply_fusion) | copy-start | bytes 7077892
  149.4 5.7 %copy-start.41 = (bf16[768,768]{1,0:T(8,128)(2,1)S(1)}, bf16[768,768]{1,0:T(8,128)(2,1)}, u32[]{:S(2)}) copy-start(bf16[768,768]{1,0:T(8,128)(2,1)} %all-gather.9.cloned.1.call-done) | copy-start | bytes 3538948
  154.1 1.0 copy-start.46
  157.3 127.1 %reduce-scatter.16.cloned.1.call-start = ((), (), s32[]{:S(2)}) async-start(), calls=%async_computation.12 | async-start | bytes 2949120
  212.9 2.0 copy-start.6
  212.9 2.0 copy-start.11
  212.9 2.0 copy-start.33
  212.9 2.0 copy-start.37
  214.9 2.4 copy-start.16
  221.5 7.9 %copy-start.10 = (bf16[2,1536,192]{1,2,0:T(8,128)(2,1)S(1)}, bf16[2,1536,192]{1,2,0:T(8,128)(2,1)}, u32[]{:S(2)}) copy-start(bf16[2,1536,192]{1,2,0:T(8,128)(2,1)} %copy-done.9) | copy-start | bytes 3538948
  221.5 7.9 %copy-start.12 = (bf16[2,384,3,64]{1,0,3,2:T(2,128)(2,1)S(1)}, bf16[2,384,3,64]{1,0,3,2:T(2,128)(2,1)}, u32[]{:S(2)}) copy-start(bf16[2,384,3,64]{1,0,3,2:T(2,128)(2,1)} %reshape.206) | copy-start | bytes 884740
  229.5 7.1 %copy-start.8 = (f32[2,384,3,64]{1,0,3,2:T(2,128)S(1)}, f32[2,384,3,64]{1,0,3,2:T(2,128)}, u32[]{:S(2)}) copy-start(f32[2,384,3,64]{1,0,3,2:T(2,128)} %copy-done.7) | copy-start | bytes 1769476
  236.6 2.9 copy-start
  251.6 77.7 %reduce-scatter.20.cloned.1.call-start = ((), (), s32[]{:S(2)}) async-start(), calls=%async_computation.14 | async-start | bytes 589824
  255.6 75.4 %reduce-scatter.22.cloned.1.call-start = ((), (), s32[]{:S(2)}) async-start(), calls=%async_computation.15 | async-start | bytes 1769472
  262.2 88.1 %reduce-scatter.18.cloned.1.call-start = ((), (), s32[]{:S(2)}) async-start(), calls=%async_computation.13 | async-start | bytes 1474560
  286.9 13.9 %copy-start.35 = (f32[768]{0:T(1024)S(1)}, f32[768]{0:T(1024)}, u32[]{:S(2)}) copy-start(f32[768]{0:T(1024)} %param.17) | copy-start | bytes 9220
  286.9 13.9 %copy-start.44 = (f32[768]{0:T(1024)S(1)}, f32[768]{0:T(1024)}, u32[]{:S(2)}) copy-start(f32[768]{0:T(1024)} %param.18) | copy-start | bytes 9220
  308.1 4.2 copy-start.38
  308.1 4.2 copy-start.45
  312.2 58.8 %reduce-scatter.14.cloned.1.call-start = ((), (), s32[]{:S(2)}) async-start(), calls=%async_computation.11 | async-start | bytes 1769472 | tf_op jit(solution)/shard_map/reduce_scatter | solution.py:228
  316.5 153.6 %all-reduce.13.cloned.1.call-start = ((), (), s32[]{:S(2)}) async-start(), calls=%async_computation.16 | async-start | bytes 4718592 | tf_op jit(solution)/shard_map/psum | solution.py:38
  316.5 3.9 copy-start.19
  316.5 3.9 copy-start.24
  322.6 198.7 %all-reduce.15.cloned.1.call-start = ((), (), s32[]{:S(2)}) async-start(), calls=%async_computation.17 | async-start | bytes 3538944 | tf_op jit(solution)/shard_map/psum | solution.py:236
  335.0 135.1 %copy-start.26 = (f32[768]{0:T(1024)S(1)}, f32[768]{0:T(1024)}, u32[]{:S(2)}) copy-start(f32[768]{0:T(1024)} %copy-done.25) | copy-start | bytes 9220
  335.0 135.1 %copy-start.28 = (f32[768]{0:T(1024)S(1)}, f32[768]{0:T(1024)}, u32[]{:S(2)}) copy-start(f32[768]{0:T(1024)} %copy-done.27) | copy-start | bytes 9220
  470.1 2.9 copy-start.5
  473.0 44.3 %copy-start.30 = (f32[768]{0:T(1024)S(1)}, f32[768]{0:T(1024)}, u32[]{:S(2)}) copy-start(f32[768]{0:T(1024)} %param.23) | copy-start | bytes 9220
  521.3 5.9 %copy-start.20 = (bf16[768,384]{1,0:T(8,128)(2,1)S(1)}, bf16[768,384]{1,0:T(8,128)(2,1)}, u32[]{:S(2)}) copy-start(bf16[768,384]{1,0:T(8,128)(2,1)} %get-tuple-element.37) | copy-start | bytes 1769476
Sparse Core Ops, SparseCore 0:
  29.4 19.0 all-gather.4
  50.6 17.5 all-gather.6
  80.7 55.8 all-reduce.8
  157.4 55.4 all-reduce.10
  251.7 32.6 reduce-scatter.15
  286.6 13.0 reduce-scatter.19
  301.9 21.7 reduce-scatter.21
  326.7 19.7 reduce-scatter.17
  349.3 21.7 reduce-scatter.13
  374.1 95.9 all-reduce.12
  472.9 46.8 all-reduce.14
Sparse Core Ops, SparseCore 1:
  82.6 22.6 all-gather.8
  106.6 22.7 all-gather.10
where the time goes:
time: 546 us; the launch traced here: 536 us
  waiting for transfers between devices  240 us (44%)
  matrix products  76.8 us (14%)
  blocking collectives  74.8 us (14%)
  local copies, waits for them, and re-layouts  67.2 us (12%)
  other arithmetic  48.6 us (9%)
  between operations  16.4 us (3%)
  starting transfers between devices  11.9 us (2%)
    psum x3, waiting for transfers between devices, tp_total(): return lax.psum(values.astype(jnp.bfloat16), 'tp').astype(jnp.float32)  197 us
    unnamed x109, local copies, waits for them, and re-layouts  43.8 us
    psum x1, blocking collectives, shards(): lax.psum((grad_g1, grad_b1, grad_ob, grad_g2, grad_b2, grad_db), ('shard'...  41 us
    reduce_scatter x1, waiting for transfers between devices, shards(): lax.psum_scatter(grad_wup.astype(jnp.bfloat16), 'shard', scatter_dimensio...  16.1 us
    psum x1, blocking collectives, shards(): vectors = lax.psum((grad_qb, grad_vb, grad_ub), ('shard', 'ctx'))  14.2 us
    all_gather x1, blocking collectives, shards(): lax.all_gather(w_qkv, 'shard', axis=1, tiled=True)  13.8 us
    unnamed x17, waiting for transfers between devices  13 us
    psum x3, starting transfers between devices, tp_total(): return lax.psum(values.astype(jnp.bfloat16), 'tp').astype(jnp.float32)  11.3 us
  transfers between devices with their start and end apart: 13, of which 7 were waited for; matrix products, arithmetic and copies ran while one was open for 22% of the time, Pallas kernels for 0%

commit v1 on v0

--- a/solution.py
+++ b/solution.py
@@ -83,7 +83,24 @@
     key_blocks = key_rows.reshape(clip_count, block_len, shard_local_width)
     value_blocks = value_rows.reshape(clip_count, block_len, shard_local_width)
     run_max = jnp.full((clip_count, heads_local, block_len), -1e30, jnp.float32)
-    key_piece = lax.all_gather(key_blocks, "ctx", axis=1, tiled=True)
+    size, here, width = (lax.axis_size("ctx"), lax.axis_index("ctx"), key_blocks.shape[1])
+    ahead = [(i, (i + 1) % size) for i in range(size)]
+    left = [(i, (i - 1) % size) for i in range(size)]
+    out = jnp.zeros(
+        (*key_blocks.shape[:1], size * width, *key_blocks.shape[1 + 1 :]), key_blocks.dtype
+    )
+    out = lax.dynamic_update_slice_in_dim(out, key_blocks, here * width, axis=1)
+    from_left = from_right = key_blocks
+    middle = size // 2
+    for hop in range(1, middle + 1):
+        from_left = lax.ppermute(from_left, "ctx", ahead)
+        out = lax.dynamic_update_slice_in_dim(out, from_left, (here - hop) % size * width, axis=1)
+        if hop < size - middle:
+            from_right = lax.ppermute(from_right, "ctx", left)
+            out = lax.dynamic_update_slice_in_dim(
+                out, from_right, (here + hop) % size * width, axis=1
+            )
+    key_piece = out
     value_piece = lax.all_gather(value_blocks, "ctx", axis=1, tiled=True)
     piece_len = key_piece.shape[1]
     key_heads = key_piece.reshape(clip_count, piece_len, heads_local, HEAD_DIM)

time: 546 us -> 541 us (level)
  starting transfers between devices: 11.9 us -> 2.58 us
  matrix products: 76.8 us -> 83.9 us
    psum x3, starting transfers between devices: 11.3 us -> 0.71 us  [tp_total(): return lax.psum(values.astype(jnp.bfloat16), 'tp').astype(jnp.float32)]
    ppermute x0 -> x3, waiting for transfers between devices: none -> 10.4 us  [the longest x2 10.4 us: shards(): from_left = lax.ppermute(from_left, 'ctx', ahead)]
    all_gather x1, waiting for transfers between devices: 10.2 us -> 0.03 us  [shards(): key_piece = lax.all_gather(key_blocks, 'ctx', axis=1, tiled=True)]
    dot_general x1 -> x2, matrix products: 7.16 us -> 14.2 us  [shards(): jnp.einsum('cqhe,cnhe->chqn', q_heads, key_heads, preferred_element_type=...]
    unnamed x109 -> x105, local copies, waits for them, and re-layouts: 43.8 us -> 45.5 us
  transfers between devices with their start and end apart: 13 -> 16, of which waited for: 7 -> 6; matrix products, arithmetic and copies ran while one was open for 22% -> 25% of each run, Pallas kernels for 0% -> 0%
where the time goes in v1:
time: 541 us; the launch traced here: 536 us
  waiting for transfers between devices  238 us (44%)
  matrix products  83.9 us (16%)
  blocking collectives  76.1 us (14%)
  local copies, waits for them, and re-layouts  70.4 us (13%)
  other arithmetic  48.5 us (9%)
  between operations  16.8 us (3%)
    psum x3, waiting for transfers between devices, tp_total(): return lax.psum(values.astype(jnp.bfloat16), 'tp').astype(jnp.float32)  198 us
    unnamed x105, local copies, waits for them, and re-layouts  45.5 us
    psum x1, blocking collectives, shards(): lax.psum((grad_g1, grad_b1, grad_ob, grad_g2, grad_b2, grad_db), ('shard'...  40.9 us
    reduce_scatter x1, waiting for transfers between devices, shards(): lax.psum_scatter(grad_wup.astype(jnp.bfloat16), 'shard', scatter_dimensio...  16 us
    psum x1, blocking collectives, shards(): vectors = lax.psum((grad_qb, grad_vb, grad_ub), ('shard', 'ctx'))  14.3 us
    dot_general x2, matrix products, shards(): jnp.einsum('cqhe,cnhe->chqn', q_heads, key_heads, preferred_element_type=...  14.2 us
    all_gather x1, blocking collectives, shards(): lax.all_gather(w_qkv, 'shard', axis=1, tiled=True)  13.8 us
    unnamed x17, waiting for transfers between devices  13.4 us
  transfers between devices with their start and end apart: 16, of which 6 were waited for; matrix products, arithmetic and copies ran while one was open for 25% of the time, Pallas kernels for 0%

profile of v1, /device:TPU:0, one launch (start us, length us, event | category | flops | bytes accessed | tf_op | source)
XLA Modules:
  0.0 536.0 jit_solution(10548772501228671356)
XLA Ops:
  8.1 1.6 convert_reduce_fusion
  9.7 1.7 fusion.23
  11.5 13.8 %all_gather.23 = bf16[3,768,192]{1,2,0:T(8,128)(2,1)S(1)} all-gather(bf16[3,384,192]{1,2,0:T(8,128)(2,1)S(1)} %copy-done.23), channel_id=1, replica_groups=mesh['shard'=2,'ctx'=4,'tp'=4] {'shard'}, dimensions={1}, use_global_device_ids=true | all-gather | bytes 1327104 | tf_op jit(solution)/shard_map/all_gather | solution.py:67
  32.6 7.0 %all_gather.25 = bf16[192,768]{1,0:T(8,128)(2,1)S(1)} all-gather(bf16[192,384]{1,0:T(8,128)(2,1)S(1)} %copy-done.24), channel_id=1, replica_groups=mesh['shard'=2,'ctx'=4,'tp'=4] {'shard'}, dimensions={1}, use_global_device_ids=true | all-gather | bytes 442368 | tf_op jit(solution)/shard_map/all_gather | solution.py:68
  42.2 10.4 %collective-permute-done.2 = bf16[2,384,192]{1,0,2:T(2,128)(2,1)S(1)} collective-permute-done((bf16[2,384,192]{1,0,2:T(2,128)(2,1)}, bf16[2,384,192]{1,0,2:T(2,128)(2,1)S(1)}, u32[]{:S(2)}, u32[]{:S(2)}) %collective-permute-start.2) | collective-permute-done | bytes 294944 | tf_op jit(solution)/shard_map/ppermute | solution.py:96
  52.7 7.1 %multiply_reduce_fusion = (f32[2,3,384]{2,1,0:T(4,128)S(1)}, f32[2,3,384,1536]{3,2,1,0:T(8,128)}) fusion(bf16[2,384,3,64]{1,3,2,0:T(8,128)(2,1)S(1)} %fusion.41, bf16[2,1536,3,64]{1,3,2,0:T(8,128)(2,1)S(1)} %bitcast.121), kind=kOutput, calls=%fused_computation.3 | convolution fusion | flops 460060416 | bytes 15639552 | tf_op jit(solution)/shard_map/cqhe,cnhe->chqn/dot_general | solution.py:109
  60.3 7.5 %fusion = f32[2,3,384]{2,1,0:T(4,128)S(1)} fusion(f32[2,3,384,1536]{3,2,1,0:T(8,128)} %get-tuple-element.45, f32[2,3,384]{2,1,0:T(4,128)S(1)} %broadcast_maximum_fusion), kind=kLoop, calls=%fused_computation.4 | loop fusion | flops 10614528 | bytes 14174208 | tf_op jit(solution)/shard_map/reduce_sum | solution.py:114
  69.3 9.0 %fusion.53 = (bf16[2,384,3,64]{1,3,2,0:T(8,128)(2,1)S(1)}, f32[2,384,3,64]{1,3,2,0:T(8,128)}) fusion(f32[2,384,3]{1,2,0:T(4,128)S(1)} %bitcast.143, bf16[2,1536,3,64]{1,3,2,0:T(8,128)(2,1)S(1)} %bitcast.119, f32[2,3,384,1536]{3,2,1,0:T(8,128)} %get-tuple-element.45, f32[2,3,384]{2,1,0:T(4,128)S(1)} %broadcast_maximum_fusion), kind=kOutput, calls=%fused_computation.117 | convolution fusion | flops 463896576 | bytes 16238592 | tf_op jit(solution)/shard_map/chqn,cnhe->chqe/dot_general | solution.py:115
  79.4 1.5 convolution_convert_fusion.4
  83.3 53.7 %all-reduce.9.cloned.1.call-done = bf16[768,768]{1,0:T(8,128)(2,1)} async-done(((bf16[768,768]{1,0:T(8,128)(2,1)}), bf16[768,768]{1,0:T(8,128)(2,1)}) %all-reduce.9.cloned.1.call-update) | async-done | bytes 1179664 | tf_op jit(solution)/shard_map/psum | solution.py:38
  137.0 1.9 fusion.33
  140.2 9.1 %fusion.15 = (bf16[768,768]{1,0:T(8,128)(2,1)}, f32[768,768]{1,0:T(8,128)}) fusion(f32[768]{0:T(1024)} %param.27, bf16[768,768]{1,0:T(8,128)(2,1)} %all-gather.7.cloned.1.call-done, f32[768,768]{1,0:T(8,128)S(1)} %subtract_multiply_fusion, f32[768]{0:T(1024)} %param.25, f32[768]{0:T(1024)} %param.24), kind=kOutput, calls=%fused_computation.18 | convolution fusion | flops 946667520 | bytes 7087104 | tf_op jit(solution)/shard_map/dot_general | solution.py:130
  149.3 4.7 convert_reduce_fusion.1
  155.0 2.1 convolution_convert_fusion.2
  160.6 7.1 %fusion.54 = f32[2,3,384,1536]{3,2,1,0:T(8,128)} fusion(bf16[2,384,3,64]{1,3,2,0:T(8,128)(2,1)S(1)} %copy-done.8, bf16[2,1536,3,64]{1,3,2,0:T(8,128)(2,1)S(1)} %bitcast.113), kind=kOutput, calls=%fused_computation.118 | convolution fusion | flops 452984832 | bytes 15630336 | tf_op jit(solution)/shard_map/cqhe,cnhe->chqn/dot_general | solution.py:171
  167.7 45.0 %all-reduce.11.cloned.1.call-done = bf16[768,768]{1,0:T(8,128)(2,1)} async-done(((bf16[768,768]{1,0:T(8,128)(2,1)}), bf16[768,768]{1,0:T(8,128)(2,1)}) %all-reduce.11.cloned.1.call-update) | async-done | bytes 1179664 | tf_op jit(solution)/shard_map/psum | solution.py:38
  212.7 1.9 multiply_reduce_fusion.5
  214.7 2.4 multiply_add_fusion
  218.4 1.7 reshape.209
  221.4 7.9 %fusion.9 = bf16[2,3,64,1536]{3,2,1,0:T(8,128)(2,1)S(1)} fusion(f32[2,3,384,1536]{3,2,1,0:T(8,128)} %fusion.54, f32[2,3,384]{2,1,0:T(4,128)S(1)} %log_add_fusion, bf16[2,384,3,64]{1,0,3,2:T(2,128)(2,1)} %reshape.209), kind=kOutput, calls=%fused_computation.14 | convolution fusion | flops 464191488 | bytes 15639552 | tf_op jit(solution)/shard_map/chqn,cqhe->cnhe/dot_general | solution.py:187
  229.4 7.0 %multiply_convert_fusion = bf16[2,3,384,1536]{3,2,1,0:T(8,128)(2,1)S(1)} fusion(f32[2,3,384,1536]{3,2,1,0:T(8,128)} %fusion.54, bf16[2,1536,3,64]{1,3,2,0:T(8,128)(2,1)S(1)} %bitcast.120, f32[2,3,384]{2,1,0:T(4,128)S(1)} %bitcast.142, f32[2,3,384]{2,1,0:T(4,128)S(1)} %log_add_fusion, bf16[2,384,3,64]{1,0,3,2:T(2,128)(2,1)S(1)} %copy-done.13), kind=kOutput, calls=%fused_computation | convolution fusion | flops 470679552 | bytes 22726656 | tf_op jit(solution)/shard_map/cqhe,cnhe->chqn/dot_general | solution.py:175
  237.8 1.5 copy-done
  239.3 1.6 pad_maximum_fusion
  241.0 6.9 %copy.67 = bf16[2,1536,384]{2,0,1:T(2,128)(2,1)} copy(bf16[2,1536,384]{1,2,0:T(8,128)(2,1)} %pad_maximum_fusion) | data formatting | bytes 4718592
  247.9 3.6 copy.80
  251.6 2.1 convolution_convert_fusion.5
  253.6 1.9 copy.71
  255.6 4.1 convolution_convert_fusion
  259.7 2.4 copy.73
  262.4 5.6 %convert_reduce_fusion.3 = (f32[3,64]{1,0:T(4,128)S(1)}, bf16[2,3,384,64]{2,3,1,0:T(8,128)(2,1)S(1)}) fusion(bf16[2,3,384,1536]{3,2,1,0:T(8,128)(2,1)} %copy-done, bf16[2,1536,3,64]{1,3,2,0:T(8,128)(2,1)} %bitcast.114), kind=kOutput, calls=%fused_computation.82 | convolution fusion | flops 453574464 | bytes 8553216 | tf_op jit(solution)/shard_map/chqn,cnhe->chqe/dot_general | solution.py:180
  269.1 1.9 convert_element_type.198
  270.9 1.7 constant_dynamic-update-slice_fusion.2
  272.6 11.7 %reduce-scatter.16.cloned.1.call-done = bf16[384,768]{1,0:T(8,128)(2,1)} async-done(((bf16[1536,768]{1,0:T(8,128)(2,1)}), bf16[384,768]{1,0:T(8,128)(2,1)}) %reduce-scatter.16.cloned.1.call-update) | async-done | bytes 589840
  284.3 2.5 reshape.219
  286.8 2.7 fusion.52
  289.5 2.0 copy.65
  291.5 1.9 convert_element_type.200
  293.3 2.0 copy.66
  295.3 1.9 convert_element_type.201
  297.2 1.7 constant_dynamic-update-slice_fusion.1
  298.9 1.7 constant_dynamic-update-slice_fusion
  300.6 2.8 fusion.44
  304.4 3.5 copy.69
  307.9 4.1 reshape.220
  312.1 4.1 convolution_convert_fusion.1
  316.3 3.9 convolution_convert_fusion.3
  320.2 2.1 bitcast_convert_fusion
  322.4 1.5 bitcast_convert_fusion.1
  327.3 1.8 dynamic-slice_reduce_fusion.2
  329.1 1.7 copy.72
  330.8 2.1 copy.74
  332.9 1.9 copy.76
  335.9 14.3 %all-reduce.1 = (f32[192]{0:T(256)}, f32[192]{0:T(256)}, f32[768]{0:T(1024)}) all-reduce(f32[192]{0:T(256)} %reduce_sum.186, f32[192]{0:T(256)S(1)} %convert_reduce_fusion.2, f32[768]{0:T(1024)} %get-tuple-element.52), channel_id=1, replica_groups=mesh['shard'=2,'ctx'=4,'tp'=4] {'shard','ctx'}, use_global_device_ids=true, to_apply=%region_23.24 | all-reduce | flops 1152 | bytes 9216 | tf_op jit(solution)/shard_map/psum | solution.py:258
  350.2 2.5 reshape.221
  352.8 2.1 copy.70
  354.9 16.0 %reduce-scatter.14.cloned.1.call-done = bf16[384,768]{1,0:T(8,128)(2,1)} async-done(((bf16[768,768]{1,0:T(8,128)(2,1)}), bf16[384,768]{1,0:T(8,128)(2,1)}) %reduce-scatter.14.cloned.1.call-update) | async-done | bytes 589840 | tf_op jit(solution)/shard_map/reduce_scatter | solution.py:245
  370.9 99.1 %all-reduce.13.cloned.1.call-done = (bf16[768,768]{1,0:T(8,128)(2,1)}, bf16[768,768]{1,0:T(8,128)(2,1)}) async-done(((bf16[768,768]{1,0:T(8,128)(2,1)}, bf16[768,768]{1,0:T(8,128)(2,1)}), (bf16[768,768]{1,0:T(8,128)(2,1)}, bf16[768,768]{1,0:T(8,128)(2,1)})) %all-reduce.13.cloned.1.call-update) | async-done | bytes 2359312 | tf_op jit(solution)/shard_map/psum | solution.py:38
  470.0 2.9 multiply_reduce_fusion.4
  473.0 1.8 dynamic-slice_reduce_fusion.3
  474.8 40.9 %all-reduce = (f32[768]{0:T(1024)}, f32[768]{0:T(1024)}, f32[768]{0:T(1024)}, f32[768]{0:T(1024)}, f32[768]{0:T(1024)}, /*index=5*/f32[768]{0:T(1024)}) all-reduce(f32[768]{0:T(1024)} %get-tuple-element.18, f32[768]{0:T(1024)} %get-tuple-element.17, ...), channel_id=1, replica_groups=mesh['shard'=2,'ctx'=4,'tp'=4] {'shard','ctx','tp'}, use_global_device_ids=true, to_apply=%region_17.18 | all-reduce | flops 4608 | bytes 36864 | tf_op jit(solution)/shard_map/psum | solution.py:259
  517.1 4.1 add_convert_fusion
  521.2 1.7 convert_element_type.211
  522.9 2.0 convert_element_type.207
  524.9 2.2 convert_element_type.213
  (172 shorter events, 34.6 us)
Async XLA Ops:
  8.0 17.3 %copy-start.1 = (bf16[2,384,768]{2,1,0:T(8,128)(2,1)S(1)}, bf16[2,384,768]{2,1,0:T(8,128)(2,1)}, u32[]{:S(2)}) copy-start(bf16[2,384,768]{2,1,0:T(8,128)(2,1)} %param.15) | copy-start | bytes 3538948
  8.0 3.5 copy-start.23
  8.0 59.8 %all-gather.5.cloned.1.call-start = ((), (), s32[]{:S(2)}) async-start(), calls=%async_computation.5 | async-start | bytes 1474560 | tf_op jit(solution)/shard_map/all_gather | solution.py:104
  11.5 14.2 %copy-start.27 = (f32[768]{0:T(1024)}, f32[768]{0:T(1024)S(1)}, u32[]{:S(2)}) copy-start(f32[768]{0:T(1024)S(1)} %rsqrt.20) | copy-start | bytes 9220
  11.5 14.2 %copy-start.34 = (f32[768]{0:T(1024)S(1)}, f32[768]{0:T(1024)}, u32[]{:S(2)}) copy-start(f32[768]{0:T(1024)} %param.17) | copy-start | bytes 9220
  11.5 14.2 %copy-start.42 = (f32[768]{0:T(1024)S(1)}, f32[768]{0:T(1024)}, u32[]{:S(2)}) copy-start(f32[768]{0:T(1024)} %param.18) | copy-start | bytes 9220
  25.3 1.3 copy-start.20
  25.7 1.4 copy-start.14
  27.2 1.2 copy-start.19
  28.4 2.4 copy-start.39
  28.5 4.0 copy-start.18
  28.5 3.4 copy-start.38
  28.5 12.7 %collective-permute-start.1 = (bf16[2,384,192]{1,0,2:T(2,128)(2,1)S(1)}, bf16[2,384,192]{1,0,2:T(2,128)(2,1)}, u32[]{:S(2)}, u32[]{:S(2)}) collective-permute-start(bf16[2,384,192]{1,0,2:T(2,128)(2,1)S(1)} %convert_element_type.177), channel_id=1, source_target_pairs={{0,12},{4,0},{8,4},{12,8},{1,13},{5,1},{9,5},{13,9},{2,14},{6,2},{... | collective-permute-start | bytes 884744 | tf_op jit(solution)/shard_map/ppermute | solution.py:99
  28.9 10.8 %collective-permute-start = (bf16[2,384,192]{1,0,2:T(2,128)(2,1)S(1)}, bf16[2,384,192]{1,0,2:T(2,128)(2,1)}, u32[]{:S(2)}, u32[]{:S(2)}) collective-permute-start(bf16[2,384,192]{1,0,2:T(2,128)(2,1)S(1)} %convert_element_type.177), channel_id=1, source_target_pairs={{0,4},{4,8},{8,12},{12,0},{1,5},{5,9},{9,13},{13,1},{2,6},{6,10},{... | collective-permute-start | bytes 884744 | tf_op jit(solution)/shard_map/ppermute | solution.py:96
  30.7 1.9 copy-start.24
  31.8 105.2 %all-reduce.9.cloned.1.call-start = ((), (), s32[]{:S(2)}) async-start(), calls=%async_computation.6 | async-start | bytes 2359296 | tf_op jit(solution)/shard_map/psum | solution.py:38
  32.4 27.3 %copy-start.7 = (bf16[2,384,3,64]{1,3,2,0:T(8,128)(2,1)}, bf16[2,384,3,64]{1,3,2,0:T(8,128)(2,1)S(1)}, u32[]{:S(2)}) copy-start(bf16[2,384,3,64]{1,3,2,0:T(8,128)(2,1)S(1)} %fusion.41) | copy-start | bytes 884740
  39.6 39.0 %copy-start.15 = (bf16[192,768]{1,0:T(8,128)(2,1)}, bf16[192,768]{1,0:T(8,128)(2,1)S(1)}, u32[]{:S(2)}) copy-start(bf16[192,768]{1,0:T(8,128)(2,1)S(1)} %all_gather.25) | copy-start | bytes 884740
  39.7 12.9 %collective-permute-start.2 = (bf16[2,384,192]{1,0,2:T(2,128)(2,1)}, bf16[2,384,192]{1,0,2:T(2,128)(2,1)S(1)}, u32[]{:S(2)}, u32[]{:S(2)}) collective-permute-start(bf16[2,384,192]{1,0,2:T(2,128)(2,1)} %collective-permute-done), channel_id=1, source_target_pairs={{0,4},{4,8},{8,12},{12,0},{1,5},{5,9},{9,13},{13,1},{2,6},{6,10},{... | collective-permute-start | bytes 884744 | tf_op jit(solution)/shard_map/ppermute | solution.py:96
  59.7 0.6 copy-start.25
  67.8 10.4 %copy-start.31 = (f32[2,3,384]{2,1,0:T(4,128)}, f32[2,3,384]{2,1,0:T(4,128)S(1)}, u32[]{:S(2)}) copy-start(f32[2,3,384]{2,1,0:T(4,128)S(1)} %fusion) | copy-start | bytes 27652
  69.3 9.0 %copy-start.10 = (bf16[2,1536,192]{1,2,0:T(8,128)(2,1)}, bf16[2,1536,192]{1,2,0:T(8,128)(2,1)S(1)}, u32[]{:S(2)}) copy-start(bf16[2,1536,192]{1,2,0:T(8,128)(2,1)S(1)} %copy.58) | copy-start | bytes 3538948
  78.6 0.8 copy-start.17
  78.6 58.4 %copy-start.29 = (f32[768]{0:T(1024)S(1)}, f32[768]{0:T(1024)}, u32[]{:S(2)}) copy-start(f32[768]{0:T(1024)} %param.23) | copy-start | bytes 9220
  81.0 59.2 %all-gather.7.cloned.1.call-start = ((), (), s32[]{:S(2)}) async-start(), calls=%async_computation.7 | async-start | bytes 1769472 | tf_op jit(solution)/shard_map/all_gather | solution.py:69
  81.5 67.8 %all-gather.9.cloned.1.call-start = ((), (), s32[]{:S(2)}) async-start(), calls=%async_computation.8 | async-start | bytes 1769472 | tf_op jit(solution)/shard_map/all_gather | solution.py:70
  82.1 76.0 %all-gather.11.cloned.1.call-start = ((), (), s32[]{:S(2)}) async-start(), calls=%async_computation.10 | async-start | bytes 1474560 | tf_op jit(solution)/shard_map/all_gather | solution.py:165
  82.7 130.0 %all-reduce.11.cloned.1.call-start = ((), (), s32[]{:S(2)}) async-start(), calls=%async_computation.9 | async-start | bytes 2359296 | tf_op jit(solution)/shard_map/psum | solution.py:38
  137.0 1.9 copy-start.3
  139.6 0.6 copy-start.32
  140.2 72.6 %copy-start.2 = (f32[768,768]{1,0:T(8,128)}, f32[768,768]{1,0:T(8,128)S(1)}, u32[]{:S(2)}) copy-start(f32[768,768]{1,0:T(8,128)S(1)} %subtract_multiply_fusion) | copy-start | bytes 7077892
  140.2 9.1 %copy-start.41 = (f32[768]{0:T(1024)S(1)}, f32[768]{0:T(1024)}, u32[]{:S(2)}) copy-start(f32[768]{0:T(1024)} %param.27) | copy-start | bytes 9220
  149.3 5.7 %copy-start.40 = (bf16[768,768]{1,0:T(8,128)(2,1)S(1)}, bf16[768,768]{1,0:T(8,128)(2,1)}, u32[]{:S(2)}) copy-start(bf16[768,768]{1,0:T(8,128)(2,1)} %all-gather.7.cloned.1.call-done) | copy-start | bytes 3538948
  154.0 1.0 copy-start.44
  157.2 127.1 %reduce-scatter.16.cloned.1.call-start = ((), (), s32[]{:S(2)}) async-start(), calls=%async_computation.12 | async-start | bytes 2949120
  158.1 2.5 copy-start.8
  159.6 1.0 copy-start.6
  212.7 2.0 copy-start.5
  212.7 2.0 copy-start.12
  212.7 2.0 copy-start.33
  212.7 2.0 copy-start.36
  214.7 2.4 copy-start.16
  221.4 7.9 %copy-start.11 = (bf16[2,1536,192]{1,2,0:T(8,128)(2,1)S(1)}, bf16[2,1536,192]{1,2,0:T(8,128)(2,1)}, u32[]{:S(2)}) copy-start(bf16[2,1536,192]{1,2,0:T(8,128)(2,1)} %copy-done.10) | copy-start | bytes 3538948
  221.4 7.9 %copy-start.13 = (bf16[2,384,3,64]{1,0,3,2:T(2,128)(2,1)S(1)}, bf16[2,384,3,64]{1,0,3,2:T(2,128)(2,1)}, u32[]{:S(2)}) copy-start(bf16[2,384,3,64]{1,0,3,2:T(2,128)(2,1)} %reshape.209) | copy-start | bytes 884740
  229.3 7.1 %copy-start.9 = (bf16[2,384,3,64]{1,3,2,0:T(8,128)(2,1)S(1)}, bf16[2,384,3,64]{1,3,2,0:T(8,128)(2,1)}, u32[]{:S(2)}) copy-start(bf16[2,384,3,64]{1,3,2,0:T(8,128)(2,1)} %copy-done.7) | copy-start | bytes 884740
  236.4 2.9 copy-start
  251.5 77.5 %reduce-scatter.20.cloned.1.call-start = ((), (), s32[]{:S(2)}) async-start(), calls=%async_computation.14 | async-start | bytes 589824
  255.5 75.2 %reduce-scatter.22.cloned.1.call-start = ((), (), s32[]{:S(2)}) async-start(), calls=%async_computation.15 | async-start | bytes 1769472
  262.2 88.1 %reduce-scatter.18.cloned.1.call-start = ((), (), s32[]{:S(2)}) async-start(), calls=%async_computation.13 | async-start | bytes 1474560
  286.8 13.8 %copy-start.35 = (f32[768]{0:T(1024)S(1)}, f32[768]{0:T(1024)}, u32[]{:S(2)}) copy-start(f32[768]{0:T(1024)} %param.17) | copy-start | bytes 9220
  286.8 13.8 %copy-start.43 = (f32[768]{0:T(1024)S(1)}, f32[768]{0:T(1024)}, u32[]{:S(2)}) copy-start(f32[768]{0:T(1024)} %param.18) | copy-start | bytes 9220
  307.9 4.2 copy-start.37
  312.0 58.8 %reduce-scatter.14.cloned.1.call-start = ((), (), s32[]{:S(2)}) async-start(), calls=%async_computation.11 | async-start | bytes 1769472 | tf_op jit(solution)/shard_map/reduce_scatter | solution.py:245
  316.2 153.8 %all-reduce.13.cloned.1.call-start = ((), (), s32[]{:S(2)}) async-start(), calls=%async_computation.16 | async-start | bytes 4718592 | tf_op jit(solution)/shard_map/psum | solution.py:38
  316.3 3.9 copy-start.21
  316.3 3.9 copy-start.26
  322.4 198.8 %all-reduce.15.cloned.1.call-start = ((), (), s32[]{:S(2)}) async-start(), calls=%async_computation.17 | async-start | bytes 3538944 | tf_op jit(solution)/shard_map/psum | solution.py:253
  334.8 135.2 %copy-start.28 = (f32[768]{0:T(1024)S(1)}, f32[768]{0:T(1024)}, u32[]{:S(2)}) copy-start(f32[768]{0:T(1024)} %copy-done.27) | copy-start | bytes 9220
  470.0 2.9 copy-start.4
  472.9 44.3 %copy-start.30 = (f32[768]{0:T(1024)S(1)}, f32[768]{0:T(1024)}, u32[]{:S(2)}) copy-start(f32[768]{0:T(1024)} %param.23) | copy-start | bytes 9220
  521.2 5.9 %copy-start.22 = (bf16[768,384]{1,0:T(8,128)(2,1)S(1)}, bf16[768,384]{1,0:T(8,128)(2,1)}, u32[]{:S(2)}) copy-start(bf16[768,384]{1,0:T(8,128)(2,1)} %get-tuple-element.37) | copy-start | bytes 1769476
Sparse Core Ops, SparseCore 0:
  31.9 22.2 all-gather.4
  81.1 55.8 all-reduce.8
  157.3 55.4 all-reduce.10
  251.6 32.5 reduce-scatter.15
  286.5 13.1 reduce-scatter.19
  301.7 21.7 reduce-scatter.21
  326.4 19.7 reduce-scatter.17
  349.1 21.7 reduce-scatter.13
  374.0 95.9 all-reduce.12
  472.7 46.8 all-reduce.14
Sparse Core Ops, SparseCore 1:
  83.0 22.6 all-gather.6
  107.0 22.7 all-gather.8
  131.8 17.4 all-gather.10
